TPU v7x, 256 devices: a whole 4x4x8 slice. The times are simulated.
256 devices in a mesh: group: 4 (over x), tile: 32 (over z, y), video: 2 (over core).
Axes of the slice: x: 4, y: 4, z: 8, core: 2. Of those that a mesh axis runs over, the one named last changes fastest.
Arguments:
- features: bfloat16 [64, 8, 16, 24, 384], P(('video', 'tile'), 'group'), parts along dimension 0, may hold values from -6 to 6
- group_slot: int32 [4], replicated, may hold values from 0 to 3, each once
- margins: int32 [32, 4], P('tile'), may hold values from 0 to 4, as said below
- norm_gain: float32 [384], replicated, may hold values from 0.1 to 1.9
- kernel: bfloat16 [3, 3, 3, 384, 384], replicated, may hold values from -0.0625 to 0.0625
- conv_bias: float32 [384], replicated, may hold values from -3 to 3
Outputs:
- decoded: bfloat16 [64, 8, 16, 24, 384], P(('video', 'tile'), 'group'), parts along dimension 0
There are 2 independent parts, one for each index of `video`. A program takes and returns all parts, laid end to end along the dimension named above; an argument that names none is the same for every part. Nothing has to cross between parts.
Inputs may be any that keep to these rules, and one draw needn't show every extreme that they name: group_slot is a permutation of 0 to 3. margins[t] is (left, right, up, down) of tile t; a margin is 0 exactly at the image's border and 1 to 4 elsewhere; the margin a tile has toward a neighbour equals the neighbour's margin back; left and right margins depend only on the tile's column, up and down margins are the same for all columns; some margin equals 4.
All inputs are finite; a program needn't handle non-finite values.
Results may differ from a plain program's by a relative error of at most 0.0043.
Values may be sent and summed in bfloat16 or wider, within the bound.
No kernel may reach another device: no remote copies, remote signals or barrier semaphores. Data moves between devices by JAX's collectives and lax.ppermute only.
A program may use at most 128 MiB of HBM per device.

v0:
```python
import jax
import jax.numpy as jnp
from jax import lax
from jax.sharding import PartitionSpec as P

M = 4
GRID_R = 2


def passed_along(shard, axis, by):
    peers = lax.axis_size(axis)
    pairs = [(i, i + by) for i in range(peers) if 0 <= i + by < peers]
    return lax.ppermute(shard, axis, pairs)


def activate(values, norm_gain):
    widened = values.astype(jnp.float32)
    inv_norm = lax.rsqrt(jnp.mean(widened * widened, axis=-1, keepdims=True) + 1e-06)
    return jax.nn.silu(widened * inv_norm * norm_gain).astype(jnp.bfloat16)


def convolve(padded, kernel, conv_bias, row_count, col_count):
    frame_count = padded.shape[0] - 2
    channels = padded.shape[-1]
    summed = jnp.zeros((frame_count * row_count * col_count, kernel.shape[-1]), jnp.float32)
    for tap_time in range(3):
        for tap_row in range(3):
            window = padded[tap_time : tap_time + frame_count, tap_row : tap_row + row_count]
            stacked = jnp.concatenate(
                [window[:, :, tap_col : tap_col + col_count] for tap_col in range(3)], axis=-1
            )
            flattened = stacked.reshape(frame_count * row_count * col_count, 3 * channels)
            summed = summed + jnp.dot(
                flattened,
                kernel[tap_time, tap_row].reshape(3 * channels, -1),
                preferred_element_type=jnp.float32,
            )
    return summed.reshape(frame_count, row_count, col_count, -1) + conv_bias


def window_band(core, near, far):
    position = jnp.arange(core + 2 * M, dtype=jnp.int32)
    return (position >= M - near) & (position < M + core + far)


def rim_weight(step, core, near, far):
    position = jnp.arange(core, dtype=jnp.int32)
    if step == 1:
        distance = position + 1
        margin = near
    elif step == -1:
        distance = core - position
        margin = far
    else:
        return jnp.ones((core,), jnp.float32)
    margin_f = margin.astype(jnp.float32)
    return jnp.maximum(margin_f + 1.0 - distance.astype(jnp.float32), 0.0) / (margin_f + 1.0)


def rim_source(step, core):
    if step == 1:
        return (core - M, M, 0)
    if step == -1:
        return (0, M, M + core)
    return (0, core, M)


def panel_source(step, core):
    if step == 1:
        return (M + core, M, 0)
    if step == -1:
        return (0, M, core - M)
    return (M, core, 0)


def blend_add(weighted, weight_sum, panel, step_r, step_c, row_dest, col_dest, reaches):
    core_h = weighted.shape[1]
    core_w = weighted.shape[2]
    row_len = panel.shape[1]
    col_len = panel.shape[2]
    placed = jnp.pad(
        panel.astype(jnp.float32),
        (
            (0, 0),
            (row_dest, core_h - row_dest - row_len),
            (col_dest, core_w - col_dest - col_len),
            (0, 0),
        ),
    )
    weight = (
        rim_weight(step_r, core_h, reaches[2], reaches[3])[:, None]
        * rim_weight(step_c, core_w, reaches[0], reaches[1])[None, :]
    )
    return (weighted + placed * weight[None, :, :, None], weight_sum + weight)


def gather_rims(source_block, grid_cols):
    core_h = source_block.shape[1]
    core_w = source_block.shape[2]
    result = jnp.pad(source_block, ((0, 0), (M, M), (M, M), (0, 0)))
    for step_r in (1, 0, -1):
        for step_c in (1, 0, -1):
            if step_r == 0 and step_c == 0:
                continue
            row_first, row_len, row_dest = rim_source(step_r, core_h)
            col_first, col_len, col_dest = rim_source(step_c, core_w)
            outgoing = source_block[
                :, row_first : row_first + row_len, col_first : col_first + col_len
            ]
            incoming = passed_along(outgoing, "tile", step_r * grid_cols + step_c)
            result = result.at[:, row_dest : row_dest + row_len, col_dest : col_dest + col_len].set(
                incoming
            )
    return result


def local(features, group_slot, margins, norm_gain, kernel, conv_bias):
    own_block = features[0]
    frame_count, core_h, core_w, channels = own_block.shape
    grid_cols = lax.axis_size("tile") // GRID_R
    reaches = margins[0]
    wanted = group_slot[lax.axis_index("group")] - 1
    chosen = jnp.zeros((2, core_h, core_w, channels), jnp.bfloat16)
    pieces = lax.all_gather(own_block[None], "group", axis=0, tiled=True)
    first_dev = jnp.int32(0)
    for offset in range(pieces.shape[0]):
        matches = group_slot[first_dev + offset] == wanted
        chosen = chosen + jnp.where(matches, pieces[offset], jnp.zeros_like(pieces[offset]))
    buffered = gather_rims(jnp.concatenate([chosen, own_block], axis=0), grid_cols)
    activated = activate(buffered, norm_gain)
    padded = jnp.pad(activated, ((0, 0), (1, 1), (1, 1), (0, 0)))
    weighted = jnp.zeros((frame_count, core_h, core_w, channels), jnp.float32)
    weight_sum = jnp.zeros((core_h, core_w), jnp.float32)
    inside = (
        window_band(core_h, reaches[2], reaches[3])[:, None]
        & window_band(core_w, reaches[0], reaches[1])[None, :]
    )
    inside = jnp.pad(inside, 1)
    masked = jnp.where(inside[None, :, :, None], padded, jnp.zeros_like(padded))
    outputs = convolve(masked, kernel, conv_bias, core_h + 2 * M, core_w + 2 * M).astype(
        jnp.bfloat16
    )
    for step_r in (1, 0, -1):
        for step_c in (1, 0, -1):
            row_first, row_len, row_dest = panel_source(step_r, core_h)
            col_first, col_len, col_dest = panel_source(step_c, core_w)
            outgoing = outputs[:, row_first : row_first + row_len, col_first : col_first + col_len]
            if step_r == 0 and step_c == 0:
                incoming = outgoing
            else:
                incoming = passed_along(outgoing, "tile", step_r * grid_cols + step_c)
            weighted, weight_sum = blend_add(
                weighted, weight_sum, incoming, step_r, step_c, row_dest, col_dest, reaches
            )
    return (weighted / weight_sum[None, :, :, None]).astype(jnp.bfloat16)[None]


def solution(mesh):
    return jax.shard_map(
        local,
        mesh=mesh,
        in_specs=(
            P(("video", "tile"), "group", None, None, None),
            P(),
            P("tile", None),
            P(),
            P(),
            P(),
        ),
        out_specs=P(("video", "tile"), "group", None, None, None),
        check_vma=False,
    )
```

profile of v0, /device:TPU:32, one launch (start us, length us, event | category | flops | bytes accessed | tf_op | source)
XLA Modules:
  0.0 198.9 jit_solution(2736371241429744091)
XLA Ops:
  23.2 6.1 %fusion.21 = (bf16[1,1,3,384,384]{4,3,2,1,0:T(8,128)(2,1)}, bf16[1,1,3,384,384]{4,3,2,1,0:T(8,128)(2,1)}, bf16[1,1,3,384,384]{4,3,2,1,0:T(8,128)(2,1)}, bf16[1,1...) fusion(bf16[3,3,3,384,384]{4,3,2,1,0:T(8,128)(2,1)} %param.26), kind=kLoop, calls=%fused_computation.92 | loop fusion | bytes 15925248 | tf_op jit(solution)/shard_map/slice | solution.py:35
  29.3 18.0 %all-gather.2.cloned.1.call-done = bf16[4,2,16,24,384]{4,3,2,1,0:T(8,128)(2,1)} async-done(((bf16[1,2,16,24,384]{4,3,2,1,0:T(8,128)(2,1)}), bf16[4,2,16,24,384]{4,3,2,1,0:T(8,128)(2,1)}) %all-gather.2.cloned.1.call-update) | async-done | bytes 2359312 | tf_op jit(solution)/shard_map/all_gather | solution.py:124
  49.4 6.8 %collective-permute-start.1 = (bf16[4,4,24,384]{3,2,1,0:T(8,128)(2,1)S(1)}, bf16[4,4,24,384]{3,2,1,0:T(8,128)(2,1)S(1)}, u32[]{:S(2)}, u32[]{:S(2)}) collective-permute-start(bf16[4,4,24,384]{3,2,1,0:T(8,128)(2,1)S(1)} %get-tuple-element.150), channel_id=1, source_target_pairs={{0,32},{2,34},{4,36},{6,38},{8,40},{10,42},{12,44},{14,46},{16,48}... | collective-permute-start | bytes 884744 | tf_op jit(solution)/shard_map/ppermute | solution.py:13
  56.9 2.2 %collective-permute-start = (bf16[4,4,4,384]{3,2,1,0:T(4,128)(2,1)S(1)}, bf16[4,4,4,384]{3,2,1,0:T(4,128)(2,1)S(1)}, u32[]{:S(2)}, u32[]{:S(2)}) collective-permute-start(bf16[4,4,4,384]{3,2,1,0:T(4,128)(2,1)S(1)} %get-tuple-element.146), channel_id=1, source_target_pairs={{0,34},{2,36},{4,38},{6,40},{8,42},{10,44},{12,46},{14,48},{16,50}... | collective-permute-start | bytes 147464 | tf_op jit(solution)/shard_map/ppermute | solution.py:13
  60.6 11.7 %collective-permute-start.2 = (bf16[4,4,4,384]{3,2,1,0:T(4,128)(2,1)}, bf16[4,4,4,384]{3,2,1,0:T(4,128)(2,1)}, u32[]{:S(2)}, u32[]{:S(2)}) collective-permute-start(bf16[4,4,4,384]{3,2,1,0:T(4,128)(2,1)} %get-tuple-element.147), channel_id=1, source_target_pairs={{0,30},{2,32},{4,34},{6,36},{8,38},{10,40},{12,42},{14,44},{16,46}... | collective-permute-start | bytes 147464 | tf_op jit(solution)/shard_map/ppermute | solution.py:13
  74.4 5.0 %collective-permute-start.4 = (bf16[4,16,4,384]{3,2,1,0:T(4,128)(2,1)S(1)}, bf16[4,16,4,384]{3,2,1,0:T(4,128)(2,1)S(1)}, u32[]{:S(2)}, u32[]{:S(2)}) collective-permute-start(bf16[4,16,4,384]{3,2,1,0:T(4,128)(2,1)S(1)} %get-tuple-element.151), channel_id=1, source_target_pairs={{2,0},{4,2},{6,4},{8,6},{10,8},{12,10},{14,12},{16,14},{18,16},{20... | collective-permute-start | bytes 589832 | tf_op jit(solution)/shard_map/ppermute | solution.py:13
  83.3 2.3 %scatter.29 = bf16[4,24,32,384]{3,2,1,0:T(8,128)(2,1)S(1)} dynamic-update-slice(bf16[4,24,32,384]{3,2,1,0:T(8,128)(2,1)S(1)} %constant_dynamic-update-slice_fusion.4, bf16[4,4,24,384]{3,2,1,0:T(8,128)(2,1)S(1)} %dynamic-slice_select_fusion, s32[]{:T(128)} %constant.277.clone.1, s32[]{:T(128)} %bitcast.10, s32[]{:T(128)} %bitcast.11, s32[]{:T(128)} %constant.277.clone.1) | dynamic-update-slice | bytes 589828 | tf_op jit(solution)/shard_map/scatter | solution.py:111
  87.2 3.4 %dynamic-slice_select_fusion.1 = bf16[4,4,4,384]{3,2,1,0:T(4,128)(2,1)} fusion(bf16[4,4,4,384]{3,2,1,0:T(4,128)(2,1)} %collective-permute-done.2, bf16[4,24,32,384]{3,2,1,0:T(8,128)(2,1)S(1)} %scatter.29, s32[]{:T(128)} %bitcast.12, s32[]{:T(128)} %bitcast.13, pred[]{:T(512)} %and_reduce_fusion), kind=kLoop, calls=%fused_computation.66 | loop fusion | flops 24576 | bytes 147465 | tf_op jit(solution)/shard_map/select.10
  90.6 2.2 %scatter.30 = bf16[4,24,32,384]{3,2,1,0:T(8,128)(2,1)S(1)} dynamic-update-slice(bf16[4,24,32,384]{3,2,1,0:T(8,128)(2,1)S(1)} %scatter.29, bf16[4,4,4,384]{3,2,1,0:T(4,128)(2,1)} %dynamic-slice_select_fusion.1, s32[]{:T(128)} %constant.277.clone.1, s32[]{:T(128)} %bitcast.12, s32[]{:T(128)} %bitcast.13, s32[]{:T(128)} %constant.277.clone.1) | dynamic-update-slice | bytes 98308 | tf_op jit(solution)/shard_map/scatter | solution.py:111
  94.9 11.0 %collective-permute-done.6 = bf16[4,4,24,384]{3,2,1,0:T(8,128)(2,1)S(1)} collective-permute-done((bf16[4,4,24,384]{3,2,1,0:T(8,128)(2,1)S(1)}, bf16[4,4,24,384]{3,2,1,0:T(8,128)(2,1)S(1)}, u32[]{:S(2)}, u32[]{:S(2)}) %collective-permute-start.6) | collective-permute-done | bytes 294944 | tf_op jit(solution)/shard_map/ppermute | solution.py:13
  108.4 2.2 %fusion.7 = bf16[4,24,32,384]{3,2,1,0:T(8,128)(2,1)S(1)} fusion(bf16[4,24,32,384]{3,2,1,0:T(8,128)(2,1)S(1)} %constant_dynamic-update-slice_fusion, f32[384]{0:T(512)} %param.25, f32[4,24,32]{2,1,0:T(8,128)S(1)} %add_rsqrt_fusion), kind=kLoop, calls=%fused_computation.9 | loop fusion | flops 9437184 | bytes 4732416 | tf_op jit(solution)/shard_map/convert_element_type | solution.py:19
  112.2 4.5 %fusion.23 = (bf16[2,24,32,384]{3,2,1,0:T(8,128)(2,1)S(1)}, bf16[2,24,32,384]{3,2,1,0:T(8,128)(2,1)S(1)}, bf16[2,24,32,384]{3,2,1,0:T(8,128)(2,1)}, bf16[2,24,32...) fusion(bf16[4,26,34,384]{3,2,1,0:T(8,128)(2,1)S(1)} %pad_select, ...), kind=kLoop, calls=%fused_computation.94 | loop fusion | bytes 18874368 | tf_op jit(solution)/shard_map/slice | solution.py:30
  116.6 6.3 %fusion.22 = (bf16[2,24,32,384]{3,2,1,0:T(8,128)(2,1)}, bf16[2,24,32,384]{3,2,1,0:T(8,128)(2,1)}, bf16[2,24,32,384]{3,2,1,0:T(8,128)(2,1)}, bf16[2,24,32,384]{3,...) fusion(bf16[4,26,34,384]{3,2,1,0:T(8,128)(2,1)S(1)} %pad_select, ...), kind=kLoop, calls=%fused_computation.93 | loop fusion | bytes 44826624 | tf_op jit(solution)/shard_map/slice | solution.py:30
  123.0 3.4 %pad_maximum_fusion = (bf16[2,24,32,1152]{3,2,1,0:T(8,128)(2,1)S(1)}, bf16[2,24,32,1152]{3,2,1,0:T(8,128)(2,1)S(1)}) fusion(bf16[2,24,32,384]{3,2,1,0:T(8,128)(2,1)} %get-tuple-element.134, bf16[2,24,32,384]{3,2,1,0:T(8,128)(2,1)} %get-tuple-element.135, bf16[2,24,32,384]{3,2,1,0:T(8,128)(2,1)} %get-tuple-element.136, ...), kind=kLoop, calls=%fused_computation.10 | loop fusion | flops 21233664 | bytes 14155776 | tf_op jit(solution)/shard_map/concatenate | solution.py:29
  128.5 3.6 %convolution_add_fusion.7 = f32[1536,384]{1,0:T(8,128)} fusion(f32[1536,384]{1,0:T(8,128)S(1)} %fusion.31, bf16[1536,1152]{1,0:T(8,128)(2,1)S(1)} %bitcast.65, bf16[1152,384]{1,0:T(8,128)(2,1)S(1)} %bitcast.79), kind=kOutput, calls=%fused_computation.27 | convolution fusion | flops 1359544320 | bytes 9142272 | tf_op jit(solution)/shard_map/dot_general | solution.py:33
  135.3 3.9 %convolution_add_fusion.6 = f32[1536,384]{1,0:T(8,128)S(1)} fusion(f32[1536,384]{1,0:T(8,128)} %convolution_add_fusion.7, bf16[1536,1152]{1,0:T(8,128)(2,1)S(1)} %bitcast.66, bf16[1152,384]{1,0:T(8,128)(2,1)S(1)} %bitcast.78), kind=kOutput, calls=%fused_computation.26 | convolution fusion | flops 1359544320 | bytes 9142272 | tf_op jit(solution)/shard_map/dot_general | solution.py:33
  139.2 2.1 %convolution_add_fusion.5 = f32[1536,384]{1,0:T(8,128)S(1)} fusion(f32[1536,384]{1,0:T(8,128)S(1)} %convolution_add_fusion.6, bf16[1536,1152]{1,0:T(8,128)(2,1)S(1)} %bitcast.62, bf16[1152,384]{1,0:T(8,128)(2,1)S(1)} %bitcast.77), kind=kOutput, calls=%fused_computation.25 | convolution fusion | flops 1359544320 | bytes 9142272 | tf_op jit(solution)/shard_map/dot_general | solution.py:33
  142.6 2.2 %convolution_add_fusion.4 = f32[1536,384]{1,0:T(8,128)S(1)} fusion(f32[1536,384]{1,0:T(8,128)S(1)} %convolution_add_fusion.5, bf16[1536,1152]{1,0:T(8,128)(2,1)S(1)} %bitcast.67, bf16[1152,384]{1,0:T(8,128)(2,1)S(1)} %bitcast.76), kind=kOutput, calls=%fused_computation.24 | convolution fusion | flops 1359544320 | bytes 9142272 | tf_op jit(solution)/shard_map/dot_general | solution.py:33
  148.1 2.2 %convolution_add_fusion.2 = f32[1536,384]{1,0:T(8,128)S(1)} fusion(f32[1536,384]{1,0:T(8,128)S(1)} %convolution_add_fusion.3, bf16[1536,1152]{1,0:T(8,128)(2,1)S(1)} %bitcast.68, bf16[1152,384]{1,0:T(8,128)(2,1)S(1)} %bitcast.74), kind=kOutput, calls=%fused_computation.22 | convolution fusion | flops 1359544320 | bytes 9142272 | tf_op jit(solution)/shard_map/dot_general | solution.py:33
  159.1 9.7 %collective-permute-start.10 = (bf16[2,4,4,384]{3,2,1,0:T(4,128)(2,1)S(1)}, bf16[2,4,4,384]{3,2,1,0:T(4,128)(2,1)S(1)}, u32[]{:S(2)}, u32[]{:S(2)}) collective-permute-start(bf16[2,4,4,384]{3,2,1,0:T(4,128)(2,1)S(1)} %get-tuple-element.140), channel_id=1, source_target_pairs={{0,30},{2,32},{4,34},{6,36},{8,38},{10,40},{12,42},{14,44},{16,46}... | collective-permute-start | bytes 73736 | tf_op jit(solution)/shard_map/ppermute | solution.py:13
  168.7 3.5 %collective-permute-start.11 = (bf16[2,16,4,384]{3,2,1,0:T(4,128)(2,1)S(1)}, bf16[2,16,4,384]{3,2,1,0:T(4,128)(2,1)S(1)}, u32[]{:S(2)}, u32[]{:S(2)}) collective-permute-start(bf16[2,16,4,384]{3,2,1,0:T(4,128)(2,1)S(1)} %get-tuple-element.143), channel_id=1, source_target_pairs={{0,2},{2,4},{4,6},{6,8},{8,10},{10,12},{12,14},{14,16},{16,18},{18... | collective-permute-start | bytes 294920 | tf_op jit(solution)/shard_map/ppermute | solution.py:13
  172.3 4.4 %collective-permute-start.12 = (bf16[2,16,4,384]{3,2,1,0:T(4,128)(2,1)S(1)}, bf16[2,16,4,384]{3,2,1,0:T(4,128)(2,1)S(1)}, u32[]{:S(2)}, u32[]{:S(2)}) collective-permute-start(bf16[2,16,4,384]{3,2,1,0:T(4,128)(2,1)S(1)} %get-tuple-element.144), channel_id=1, source_target_pairs={{2,0},{4,2},{6,4},{8,6},{10,8},{12,10},{14,12},{16,14},{18,16},{20... | collective-permute-start | bytes 294920 | tf_op jit(solution)/shard_map/ppermute | solution.py:13
  180.7 3.7 %collective-permute-done.9 = bf16[2,4,24,384]{3,2,1,0:T(8,128)(2,1)S(1)} collective-permute-done((bf16[2,4,24,384]{3,2,1,0:T(8,128)(2,1)S(1)}, bf16[2,4,24,384]{3,2,1,0:T(8,128)(2,1)S(1)}, u32[]{:S(2)}, u32[]{:S(2)}) %collective-permute-start.9) | collective-permute-done | bytes 147488 | tf_op jit(solution)/shard_map/ppermute | solution.py:13
  184.4 5.5 %collective-permute-done.14 = bf16[2,4,24,384]{3,2,1,0:T(8,128)(2,1)S(1)} collective-permute-done((bf16[2,4,24,384]{3,2,1,0:T(8,128)(2,1)S(1)}, bf16[2,4,24,384]{3,2,1,0:T(8,128)(2,1)S(1)}, u32[]{:S(2)}, u32[]{:S(2)}) %collective-permute-start.14) | collective-permute-done | bytes 147488 | tf_op jit(solution)/shard_map/ppermute | solution.py:13
  (102 shorter events, 50.6 us)
Async XLA Ops:
  6.5 40.8 %all-gather.2.cloned.1.call-start = ((), (), s32[]{:S(2)}) async-start(), calls=%async_computation | async-start | bytes 2949120 | tf_op jit(solution)/shard_map/all_gather | solution.py:124
  29.3 19.8 %copy-start = (bf16[1,2,16,24,384]{4,3,2,1,0:T(8,128)(2,1)S(1)}, bf16[1,2,16,24,384]{4,3,2,1,0:T(8,128)(2,1)}, u32[]{:S(2)}) copy-start(bf16[1,2,16,24,384]{4,3,2,1,0:T(8,128)(2,1)} %param.22) | copy-start | bytes 1769476
  49.4 30.2 %collective-permute-start.1 = (bf16[4,4,24,384]{3,2,1,0:T(8,128)(2,1)S(1)}, bf16[4,4,24,384]{3,2,1,0:T(8,128)(2,1)S(1)}, u32[]{:S(2)}, u32[]{:S(2)}) collective-permute-start(bf16[4,4,24,384]{3,2,1,0:T(8,128)(2,1)S(1)} %get-tuple-element.150), channel_id=1, source_target_pairs={{0,32},{2,34},{4,36},{6,38},{8,40},{10,42},{12,44},{14,46},{16,48}... | collective-permute-start | bytes 884744 | tf_op jit(solution)/shard_map/ppermute | solution.py:13
  56.9 17.6 %collective-permute-start = (bf16[4,4,4,384]{3,2,1,0:T(4,128)(2,1)S(1)}, bf16[4,4,4,384]{3,2,1,0:T(4,128)(2,1)S(1)}, u32[]{:S(2)}, u32[]{:S(2)}) collective-permute-start(bf16[4,4,4,384]{3,2,1,0:T(4,128)(2,1)S(1)} %get-tuple-element.146), channel_id=1, source_target_pairs={{0,34},{2,36},{4,38},{6,40},{8,42},{10,44},{12,46},{14,48},{16,50}... | collective-permute-start | bytes 147464 | tf_op jit(solution)/shard_map/ppermute | solution.py:13
  59.3 47.8 %collective-permute-start.7 = (bf16[4,4,4,384]{3,2,1,0:T(4,128)(2,1)}, bf16[4,4,4,384]{3,2,1,0:T(4,128)(2,1)}, u32[]{:S(2)}, u32[]{:S(2)}) collective-permute-start(bf16[4,4,4,384]{3,2,1,0:T(4,128)(2,1)} %get-tuple-element.145), channel_id=1, source_target_pairs={{34,0},{36,2},{38,4},{40,6},{42,8},{44,10},{46,12},{48,14},{50,16}... | collective-permute-start | bytes 147464 | tf_op jit(solution)/shard_map/ppermute | solution.py:13
  60.6 25.1 %collective-permute-start.2 = (bf16[4,4,4,384]{3,2,1,0:T(4,128)(2,1)}, bf16[4,4,4,384]{3,2,1,0:T(4,128)(2,1)}, u32[]{:S(2)}, u32[]{:S(2)}) collective-permute-start(bf16[4,4,4,384]{3,2,1,0:T(4,128)(2,1)} %get-tuple-element.147), channel_id=1, source_target_pairs={{0,30},{2,32},{4,34},{6,36},{8,38},{10,40},{12,42},{14,44},{16,46}... | collective-permute-start | bytes 147464 | tf_op jit(solution)/shard_map/ppermute | solution.py:13
  72.3 21.7 %collective-permute-start.5 = (bf16[4,4,4,384]{3,2,1,0:T(4,128)(2,1)}, bf16[4,4,4,384]{3,2,1,0:T(4,128)(2,1)}, u32[]{:S(2)}, u32[]{:S(2)}) collective-permute-start(bf16[4,4,4,384]{3,2,1,0:T(4,128)(2,1)} %get-tuple-element.148), channel_id=1, source_target_pairs={{30,0},{32,2},{34,4},{36,6},{38,8},{40,10},{42,12},{44,14},{46,16}... | collective-permute-start | bytes 147464 | tf_op jit(solution)/shard_map/ppermute | solution.py:13
  74.4 19.4 %collective-permute-start.4 = (bf16[4,16,4,384]{3,2,1,0:T(4,128)(2,1)S(1)}, bf16[4,16,4,384]{3,2,1,0:T(4,128)(2,1)S(1)}, u32[]{:S(2)}, u32[]{:S(2)}) collective-permute-start(bf16[4,16,4,384]{3,2,1,0:T(4,128)(2,1)S(1)} %get-tuple-element.151), channel_id=1, source_target_pairs={{2,0},{4,2},{6,4},{8,6},{10,8},{12,10},{14,12},{16,14},{18,16},{20... | collective-permute-start | bytes 589832 | tf_op jit(solution)/shard_map/ppermute | solution.py:13
  79.5 13.3 %collective-permute-start.3 = (bf16[4,16,4,384]{3,2,1,0:T(4,128)(2,1)S(1)}, bf16[4,16,4,384]{3,2,1,0:T(4,128)(2,1)}, u32[]{:S(2)}, u32[]{:S(2)}) collective-permute-start(bf16[4,16,4,384]{3,2,1,0:T(4,128)(2,1)S(1)} %get-tuple-element.152), channel_id=1, source_target_pairs={{0,2},{2,4},{4,6},{6,8},{8,10},{10,12},{12,14},{14,16},{16,18},{18... | collective-permute-start | bytes 589832 | tf_op jit(solution)/shard_map/ppermute | solution.py:13
  85.7 20.1 %collective-permute-start.6 = (bf16[4,4,24,384]{3,2,1,0:T(8,128)(2,1)S(1)}, bf16[4,4,24,384]{3,2,1,0:T(8,128)(2,1)S(1)}, u32[]{:S(2)}, u32[]{:S(2)}) collective-permute-start(bf16[4,4,24,384]{3,2,1,0:T(8,128)(2,1)S(1)} %get-tuple-element.149), channel_id=1, source_target_pairs={{32,0},{34,2},{36,4},{38,6},{40,8},{42,10},{44,12},{46,14},{48,16}... | collective-permute-start | bytes 884744 | tf_op jit(solution)/shard_map/ppermute | solution.py:13
  123.0 3.4 %copy-start.14 = (bf16[1,1,3,384,384]{4,3,2,1,0:T(8,128)(2,1)S(1)}, bf16[1,1,3,384,384]{4,3,2,1,0:T(8,128)(2,1)}, u32[]{:S(2)}) copy-start(bf16[1,1,3,384,384]{4,3,2,1,0:T(8,128)(2,1)} %get-tuple-element.108) | copy-start | bytes 2654212
  128.5 3.7 %copy-start.2 = (bf16[2,24,32,384]{3,2,1,0:T(8,128)(2,1)S(1)}, bf16[2,24,32,384]{3,2,1,0:T(8,128)(2,1)}, u32[]{:S(2)}) copy-start(bf16[2,24,32,384]{3,2,1,0:T(8,128)(2,1)} %get-tuple-element.110) | copy-start | bytes 3538948
  128.5 3.7 %copy-start.3 = (bf16[2,24,32,384]{3,2,1,0:T(8,128)(2,1)S(1)}, bf16[2,24,32,384]{3,2,1,0:T(8,128)(2,1)}, u32[]{:S(2)}) copy-start(bf16[2,24,32,384]{3,2,1,0:T(8,128)(2,1)} %get-tuple-element.111) | copy-start | bytes 3538948
  128.5 3.6 %copy-start.4 = (bf16[2,24,32,384]{3,2,1,0:T(8,128)(2,1)S(1)}, bf16[2,24,32,384]{3,2,1,0:T(8,128)(2,1)}, u32[]{:S(2)}) copy-start(bf16[2,24,32,384]{3,2,1,0:T(8,128)(2,1)} %get-tuple-element.112) | copy-start | bytes 3538948
  135.3 3.9 %copy-start.11 = (bf16[1,1,3,384,384]{4,3,2,1,0:T(8,128)(2,1)S(1)}, bf16[1,1,3,384,384]{4,3,2,1,0:T(8,128)(2,1)}, u32[]{:S(2)}) copy-start(bf16[1,1,3,384,384]{4,3,2,1,0:T(8,128)(2,1)} %get-tuple-element.105) | copy-start | bytes 2654212
  154.6 24.9 %copy-start.15 = (f32[24]{0:T(128)S(1)}, f32[24]{0:T(128)}, u32[]{:S(2)}) copy-start(f32[24]{0:T(128)} %get-tuple-element.182) | copy-start | bytes 292
  155.1 17.2 %collective-permute-start.8 = (bf16[2,4,4,384]{3,2,1,0:T(4,128)(2,1)S(1)}, bf16[2,4,4,384]{3,2,1,0:T(4,128)(2,1)S(1)}, u32[]{:S(2)}, u32[]{:S(2)}) collective-permute-start(bf16[2,4,4,384]{3,2,1,0:T(4,128)(2,1)S(1)} %get-tuple-element.137), channel_id=1, source_target_pairs={{0,34},{2,36},{4,38},{6,40},{8,42},{10,44},{12,46},{14,48},{16,50}... | collective-permute-start | bytes 73736 | tf_op jit(solution)/shard_map/ppermute | solution.py:13
  156.4 20.3 %collective-permute-start.15 = (bf16[2,4,4,384]{3,2,1,0:T(4,128)(2,1)S(1)}, bf16[2,4,4,384]{3,2,1,0:T(4,128)(2,1)S(1)}, u32[]{:S(2)}, u32[]{:S(2)}) collective-permute-start(bf16[2,4,4,384]{3,2,1,0:T(4,128)(2,1)S(1)} %get-tuple-element.138), channel_id=1, source_target_pairs={{34,0},{36,2},{38,4},{40,6},{42,8},{44,10},{46,12},{48,14},{50,16}... | collective-permute-start | bytes 73736 | tf_op jit(solution)/shard_map/ppermute | solution.py:13
  157.7 20.5 %collective-permute-start.13 = (bf16[2,4,4,384]{3,2,1,0:T(4,128)(2,1)S(1)}, bf16[2,4,4,384]{3,2,1,0:T(4,128)(2,1)S(1)}, u32[]{:S(2)}, u32[]{:S(2)}) collective-permute-start(bf16[2,4,4,384]{3,2,1,0:T(4,128)(2,1)S(1)} %get-tuple-element.139), channel_id=1, source_target_pairs={{30,0},{32,2},{34,4},{36,6},{38,8},{40,10},{42,12},{44,14},{46,16}... | collective-permute-start | bytes 73736 | tf_op jit(solution)/shard_map/ppermute | solution.py:13
  159.1 20.5 %collective-permute-start.10 = (bf16[2,4,4,384]{3,2,1,0:T(4,128)(2,1)S(1)}, bf16[2,4,4,384]{3,2,1,0:T(4,128)(2,1)S(1)}, u32[]{:S(2)}, u32[]{:S(2)}) collective-permute-start(bf16[2,4,4,384]{3,2,1,0:T(4,128)(2,1)S(1)} %get-tuple-element.140), channel_id=1, source_target_pairs={{0,30},{2,32},{4,34},{6,36},{8,38},{10,40},{12,42},{14,44},{16,46}... | collective-permute-start | bytes 73736 | tf_op jit(solution)/shard_map/ppermute | solution.py:13
  168.7 10.9 %collective-permute-start.11 = (bf16[2,16,4,384]{3,2,1,0:T(4,128)(2,1)S(1)}, bf16[2,16,4,384]{3,2,1,0:T(4,128)(2,1)S(1)}, u32[]{:S(2)}, u32[]{:S(2)}) collective-permute-start(bf16[2,16,4,384]{3,2,1,0:T(4,128)(2,1)S(1)} %get-tuple-element.143), channel_id=1, source_target_pairs={{0,2},{2,4},{4,6},{6,8},{8,10},{10,12},{12,14},{14,16},{16,18},{18... | collective-permute-start | bytes 294920 | tf_op jit(solution)/shard_map/ppermute | solution.py:13
  172.3 8.4 %collective-permute-start.12 = (bf16[2,16,4,384]{3,2,1,0:T(4,128)(2,1)S(1)}, bf16[2,16,4,384]{3,2,1,0:T(4,128)(2,1)S(1)}, u32[]{:S(2)}, u32[]{:S(2)}) collective-permute-start(bf16[2,16,4,384]{3,2,1,0:T(4,128)(2,1)S(1)} %get-tuple-element.144), channel_id=1, source_target_pairs={{2,0},{4,2},{6,4},{8,6},{10,8},{12,10},{14,12},{16,14},{18,16},{20... | collective-permute-start | bytes 294920 | tf_op jit(solution)/shard_map/ppermute | solution.py:13
  176.7 7.7 %collective-permute-start.9 = (bf16[2,4,24,384]{3,2,1,0:T(8,128)(2,1)S(1)}, bf16[2,4,24,384]{3,2,1,0:T(8,128)(2,1)S(1)}, u32[]{:S(2)}, u32[]{:S(2)}) collective-permute-start(bf16[2,4,24,384]{3,2,1,0:T(8,128)(2,1)S(1)} %get-tuple-element.141), channel_id=1, source_target_pairs={{0,32},{2,34},{4,36},{6,38},{8,40},{10,42},{12,44},{14,46},{16,48}... | collective-permute-start | bytes 442376 | tf_op jit(solution)/shard_map/ppermute | solution.py:13
  178.2 11.7 %collective-permute-start.14 = (bf16[2,4,24,384]{3,2,1,0:T(8,128)(2,1)S(1)}, bf16[2,4,24,384]{3,2,1,0:T(8,128)(2,1)S(1)}, u32[]{:S(2)}, u32[]{:S(2)}) collective-permute-start(bf16[2,4,24,384]{3,2,1,0:T(8,128)(2,1)S(1)} %get-tuple-element.142), channel_id=1, source_target_pairs={{32,0},{34,2},{36,4},{38,6},{40,8},{42,10},{44,12},{46,14},{48,16}... | collective-permute-start | bytes 442376 | tf_op jit(solution)/shard_map/ppermute | solution.py:13
  (10 other events, 18.4 us)
Sparse Core Ops, SparseCore 0:
  9.2 38.1 all-gather.1
where the time goes:
time: 202 us; the launch traced here: 199 us
  starting transfers between devices  55.9 us (28%)
  waiting for transfers between devices  40 us (20%)
  local copies, waits for them, and re-layouts  31.8 us (16%)
  other arithmetic  26.4 us (13%)
  matrix products  22.5 us (11%)
  between operations  22.2 us (11%)
    ppermute x16, starting transfers between devices, passed_along(): return lax.ppermute(shard, axis, pairs)  55.9 us
    dot_general x9, matrix products, convolve(): jnp.dot(flattened, kernel[tap_time, tap_row].reshape(3 * channels, -1), p...  22.5 us
    ppermute x16, waiting for transfers between devices, passed_along(): return lax.ppermute(shard, axis, pairs)  21.3 us
    all_gather x1, waiting for transfers between devices, local(): pieces = lax.all_gather(own_block[None], 'group', axis=0, tiled=True)  18 us
    slice x2, local copies, waits for them, and re-layouts, convolve(): window[:, :, tap_col:tap_col + col_count]  10.8 us
    scatter x8, local copies, waits for them, and re-layouts, gather_rims(): result.at[:, row_dest:row_dest + row_len, col_dest:col_dest + col_len]  8.67 us
    another operation x6, other arithmetic  8.1 us
    concatenate x5, other arithmetic, convolve(): jnp.concatenate([window[:, :, tap_col:tap_col + col_count] for tap_col in...  8 us
  transfers between devices with their start and end apart: 17, of which 5 were waited for; matrix products, arithmetic and copies ran while one was open for 14% of the time, Pallas kernels for 0%

commit v1 on v0

v1 whole, which is shorter than its diff:
```python
import functools

import jax
import jax.numpy as jnp
from jax import lax
from jax.experimental import pallas as pl
from jax.experimental.pallas import tpu as pltpu
from jax.sharding import PartitionSpec as P

GRID_R = 2
ROWS, COLS, C = 16, 24, 384
CELLS = ROWS * COLS
PAIR = 2 * COLS
TAPS = 9
DEPTH = TAPS * C


def activated(values, gain):
    inv_norm = lax.rsqrt(jnp.mean(values * values, axis=-1, keepdims=True) + 1e-06)
    scaled = values * inv_norm * gain
    silu = 0.5 * scaled * (1.0 + jnp.tanh(0.5 * scaled))
    return silu.astype(jnp.bfloat16).astype(jnp.float32)


def blend_coef(position, tap, core, near, far):
    source = position + (tap - 1)
    near_f, far_f = near.astype(jnp.float32), far.astype(jnp.float32)
    weight_near = jnp.maximum(near - position, 0).astype(jnp.float32) / (near_f + 1.0)
    weight_far = jnp.maximum(far + 1 - core + position, 0).astype(jnp.float32) / (far_f + 1.0)
    kept = jnp.where(source < near, weight_near, 0.0)
    kept = kept + jnp.where(source >= core - far, weight_far, 0.0)
    kept = kept + jnp.where((source >= -near) & (source < core + far), 1.0, 0.0)
    return kept / (weight_near + 1.0 + weight_far)


def fill_coefs(coefs, margins):
    flat = lax.broadcasted_iota(jnp.int32, (CELLS, 128), 0)
    row = (flat * 2731) >> 16
    col = flat - row * COLS
    by_row = {b: blend_coef(row, b, ROWS, margins[0, 2], margins[0, 3]) for b in (0, 2)}
    by_col = {e: blend_coef(col, e, COLS, margins[0, 0], margins[0, 1]) for e in (0, 2)}
    for b in range(3):
        for e in range(3):
            if b == 1 and e == 1:
                continue
            if b == 1:
                coef = by_col[e]
            elif e == 1:
                coef = by_row[b]
            else:
                coef = by_row[b] * by_col[e]
            coefs[3 * b + e] = coef


def shifted(block, left, right):
    rows = block.shape[0]
    place = lax.broadcasted_iota(jnp.int32, block.shape, 0)
    before = pltpu.roll(block, 1, 0)
    after = pltpu.roll(block, rows - 1, 0)
    for n in range(rows // COLS):
        before = jnp.where(place == n * COLS, left[n], before)
        after = jnp.where(place == n * COLS + COLS - 1, right[n], after)
    return before, block, after


def expand(core, halo, gain, coefs, sides, cells, stacked, top, keep):
    zero = jnp.zeros((COLS, C), jnp.float32)
    for f in range(2):
        left = activated(halo[1, f].astype(jnp.float32), gain)
        right = activated(halo[2, f].astype(jnp.float32), gain)
        if keep is not None:
            left, right = jnp.where(keep, left, 0.0), jnp.where(keep, right, 0.0)
        sides[0, f] = left
        sides[1, f] = right
        rim = activated(halo[0, f].astype(jnp.float32), gain)
        if keep is not None:
            rim = jnp.where(keep, rim, 0.0)
        views = shifted(rim, [left[ROWS : ROWS + 1]], [right[ROWS : ROWS + 1]])
        for e in range(3):
            cells[f, e, 0:COLS] = jnp.where(top, views[e], zero)
            cells[f, e, (ROWS + 1) * COLS : (ROWS + 2) * COLS] = jnp.where(top, zero, views[e])

    for f in range(2):

        def widen(k, _):
            first = pl.multiple_of(k * PAIR, 16)
            block = core[pl.ds(pl.multiple_of(f * CELLS + k * PAIR, 16), PAIR), :]
            block = activated(block.astype(jnp.float32), gain)
            if keep is not None:
                block = jnp.where(keep, block, 0.0)
            views = shifted(
                block,
                [sides[0, f, pl.ds(2 * k + n, 1), :] for n in range(2)],
                [sides[1, f, pl.ds(2 * k + n, 1), :] for n in range(2)],
            )
            for e in range(3):
                cells[f, e, pl.ds(pl.multiple_of(first + COLS, 8), PAIR), :] = views[e]
            return 0

        lax.fori_loop(0, ROWS // 2, widen, 0)

    for f in range(2):

        def stack(k, _):
            first = pl.multiple_of(k * PAIR, 16)
            for b in range(3):
                for e in range(3):
                    block = cells[f, e, pl.ds(pl.multiple_of(first + b * COLS, 8), PAIR), :]
                    if b != 1 or e != 1:
                        coef = coefs[3 * b + e, pl.ds(first, PAIR), :]
                        block = block * jnp.concatenate([coef] * (C // 128), axis=1)
                    lanes = slice((3 * b + e) * C, (3 * b + e + 1) * C)
                    stacked[f, pl.ds(first, PAIR), lanes] = block.astype(jnp.bfloat16)
            return 0

        lax.fori_loop(0, ROWS // 2, stack, 0)


def fetch(weights, taps, sems, first, second):
    copies = [
        pltpu.make_async_copy(weights.at[a], taps.at[:, pl.ds(n * C, C)], sems.at[n])
        for n, a in enumerate((first, second))
    ]
    for copy in copies:
        copy.start()
    return copies


def dot(a, b):
    return jnp.dot(a, b, preferred_element_type=jnp.float32)


def own_kernel(margins, where, core, halo, gain, weights, out, taps, coefs, sides, cells, stacked, sems):
    copies = fetch(weights, taps, sems, 2, 1)
    fill_coefs(coefs, margins)
    expand(core, halo, gain[...], coefs, sides, cells, stacked, where[0] == 1, None)
    for copy in copies:
        copy.wait()
    out[0] = dot(stacked[0], taps[:, :C])
    out[1] = dot(stacked[0], taps[:, C:]) + dot(stacked[1], taps[:, :C])


def previous_kernel(
    margins, where, core, halo, gain, weights, own, bias, out, taps, coefs, sides, cells, stacked, sems
):
    copies = fetch(weights, taps, sems, 1, 0)
    fill_coefs(coefs, margins)
    expand(core, halo, gain[...], coefs, sides, cells, stacked, where[0] == 1, where[1] > 0)
    for copy in copies:
        copy.wait()
    first = own[0] + bias[...] + dot(stacked[1], taps[:, :C]) + dot(stacked[0], taps[:, C:])
    out[0:CELLS] = first.astype(jnp.bfloat16)
    second = own[1] + bias[...] + dot(stacked[1], taps[:, C:])
    out[CELLS : 2 * CELLS] = second.astype(jnp.bfloat16)


def call(kernel, inputs, out_shape):
    smem, vmem, hbm = (
        pl.BlockSpec(memory_space=pltpu.SMEM),
        pl.BlockSpec(memory_space=pltpu.VMEM),
        pl.BlockSpec(memory_space=pl.ANY),
    )
    specs = [smem, smem, vmem, vmem, vmem, hbm] + [vmem] * (len(inputs) - 6)
    return pl.pallas_call(
        kernel,
        in_specs=specs,
        out_specs=vmem,
        out_shape=out_shape,
        scratch_shapes=[
            pltpu.VMEM((DEPTH, 2 * C), jnp.bfloat16),
            pltpu.VMEM((TAPS, CELLS, 128), jnp.float32),
            pltpu.VMEM((2, 2, COLS, C), jnp.float32),
            pltpu.VMEM((2, 3, (ROWS + 2) * COLS, C), jnp.float32),
            pltpu.VMEM((2, CELLS, DEPTH), jnp.bfloat16),
            pltpu.SemaphoreType.DMA((2,)),
        ],
        compiler_params=pltpu.CompilerParams(vmem_limit_bytes=44 * 2**20),
        cost_estimate=pl.CostEstimate(
            flops=2 * 3 * CELLS * DEPTH * C, bytes_accessed=8 * 2**20, transcendentals=2 * CELLS * C
        ),
    )(*inputs)


def cyclic_order(index):
    place = index // 2 + 1
    others = [p for p in (1, 2, 3) if p != place]
    if index % 2:
        others = others[::-1]
    places = [0, place] + others
    return sorted(range(4), key=lambda d: places[d])


def local(features, group_slot, margins, norm_gain, kernel, conv_bias):
    tiles = lax.axis_size("tile")
    across = tiles // GRID_R
    tile = lax.axis_index("tile")
    tile_row = tile // across
    slot = group_slot[lax.axis_index("group")]
    where = jnp.stack([tile_row, slot]).astype(jnp.int32)
    weights = kernel.reshape(3, DEPTH, C)
    gain = norm_gain.reshape(1, C)
    bias = conv_bias.reshape(1, C)
    core = features.reshape(2 * CELLS, C)

    def routed(order):
        route = [(order[n], order[(n + 1) % 4]) for n in range(4)]

        def branch(features, where, margins, gain, weights):
            own = features[0]
            previous = lax.ppermute(features, "group", route)
            edge = lax.dynamic_index_in_dim(
                own, jnp.where(where[0] == 1, 0, ROWS - 1), axis=1, keepdims=False
            )
            rim = lax.ppermute(edge, "tile", [(t, (t + across) % tiles) for t in range(tiles)])
            columns = [
                jnp.pad(
                    jnp.concatenate([own[:, :, at], rim[:, at : at + 1]], axis=1),
                    ((0, 0), (0, COLS - ROWS - 1), (0, 0)),
                )
                for at in (COLS - 1, 0)
            ]
            inner = [t for t in range(tiles) if t % across != across - 1]
            left = lax.ppermute(columns[0], "tile", [(t, t + 1) for t in inner])
            right = lax.ppermute(columns[1], "tile", [(t + 1, t) for t in inner])
            halo = jnp.stack([rim, left, right])
            halo_previous = lax.ppermute(halo, "group", route)
            partial = call(
                own_kernel,
                (margins, where, own.reshape(2 * CELLS, C), halo, gain, weights),
                jax.ShapeDtypeStruct((2, CELLS, C), jnp.float32),
            )
            return previous, halo_previous, partial

        return branch

    away = (group_slot[1:] - group_slot[0]) % 4
    index = (away[0] - 1) * 2 + (away[1] > away[2]).astype(jnp.int32)
    previous, halo_previous, partial = lax.switch(
        index,
        [routed(cyclic_order(n)) for n in range(6)],
        features,
        where,
        margins,
        gain,
        weights,
    )
    decoded = call(
        previous_kernel,
        (margins, where, previous.reshape(2 * CELLS, C), halo_previous, gain, weights, partial, bias),
        jax.ShapeDtypeStruct((2 * CELLS, C), jnp.bfloat16),
    )
    return decoded.reshape(1, 2, ROWS, COLS, C)


def solution(mesh):
    return jax.shard_map(
        local,
        mesh=mesh,
        in_specs=(
            P(("video", "tile"), "group", None, None, None),
            P(),
            P("tile", None),
            P(),
            P(),
            P(),
        ),
        out_specs=P(("video", "tile"), "group", None, None, None),
        check_vma=False,
    )
```

time: 202 us -> 57.6 us (0.29)
  the two profiles are of different devices: /device:TPU:32 before, /device:TPU:24 now
where the time goes in v1:
time: 57.6 us; the launch traced here: 56.7 us
  Pallas kernels  19 us (33%)
  starting transfers between devices  18 us (31%)
  waiting for transfers between devices  6.66 us (12%)
  loops' own time  4.49 us (8%)
  local copies, waits for them, and re-layouts  4.25 us (7%)
  other arithmetic  2.18 us (4%)
  between operations  2.15 us (4%)
    pallas_call x2, Pallas kernels, call(): pl.pallas_call(kernel, in_specs=specs, out_specs=vmem, out_shape=out_shap...  19 us
    ppermute x1, starting transfers between devices, branch(): lax.ppermute(edge, 'tile', [(t, (t + across) % tiles) for t in range(tile...  7.28 us
    ppermute x1, waiting for transfers between devices, branch(): right = lax.ppermute(columns[1], 'tile', [(t + 1, t) for t in inner])  4.68 us
    another operation x1, loops' own time, local(): lax.switch(index, [routed(cyclic_order(n)) for n in range(6)], features,...  4.49 us
    ppermute x1, starting transfers between devices, branch(): right = lax.ppermute(columns[1], 'tile', [(t + 1, t) for t in inner])  3.27 us
    ppermute x1, starting transfers between devices, branch(): previous = lax.ppermute(features, 'group', route)  3.1 us
    ppermute x1, starting transfers between devices, branch(): left = lax.ppermute(columns[0], 'tile', [(t, t + 1) for t in inner])  2.58 us
    ppermute x1, waiting for transfers between devices, branch(): lax.ppermute(edge, 'tile', [(t, (t + across) % tiles) for t in range(tile...  1.97 us
  transfers between devices with their start and end apart: 5, of which 2 were waited for; matrix products, arithmetic and copies ran while one was open for 1% of the time, Pallas kernels for 16%

profile of v1, /device:TPU:24, one launch (start us, length us, event | category | flops | bytes accessed | tf_op | source)
XLA Modules:
  0.0 56.7 jit_solution(9365392011941593878)
XLA Ops:
  0.0 1.4 %fusion.44 = (s32[1]{0:T(128)}, s32[1]{0:T(128)}) fusion(s32[4]{0:T(128)} %param.13, s32[]{:T(128)S(6)} %select_n.41), kind=kLoop, calls=%fused_computation.90 | loop fusion | bytes 20 | tf_op jit(solution)/shard_map/slice | solution.py:236
  1.4 0.8 %pad_add_fusion.where = s32[2]{0:T(128)S(1)} fusion(s32[1]{0:T(128)} %get-tuple-element.196, s32[1]{0:T(128)} %bitcast.54), kind=kLoop, calls=%fused_computation.82 | loop fusion | flops 2 | bytes 16 | tf_op jit(solution)/shard_map/stack | solution.py:199
  2.2 0.7 %reshape.47.gain = f32[1,384]{1,0:T(1,128)S(1)} reshape(f32[384]{0:T(512)} %param.15) | data formatting | bytes 3072 | tf_op jit(solution)/shard_map/reshape | solution.py:201
  2.8 1.4 %and_select_fusion = s32[3]{0:T(128)S(1)} fusion(s32[4]{0:T(128)} %param.13, s32[]{:T(128)} %bitcast.55), kind=kLoop, calls=%fused_computation.80 | loop fusion | flops 36 | bytes 28 | tf_op jit(solution)/shard_map/jit(remainder)/select_n | solution.py:236
  4.2 0.7 %fusion.43 = (s32[1]{0:T(128)}, s32[1]{0:T(128)}, s32[1]{0:T(128)}) fusion(s32[3]{0:T(128)S(1)} %and_select_fusion), kind=kLoop, calls=%fused_computation.89 | loop fusion | bytes 24 | tf_op jit(solution)/shard_map/slice | solution.py:237
  6.8 0.0 copy-start.6
  6.8 39.6 %conditional.1 = (bf16[3,2,24,384]{3,2,1,0:T(8,128)(2,1)}, f32[2,384,384]{2,1,0:T(8,128)S(1)}, bf16[768,384]{1,0:T(8,128)(2,1)S(1)}) conditional(s32[]{:T(128)} %bitcast.56, (s32[]{:T(128)}, bf16[1,2,16,24,384]{4,3,2,1,0:T(8,128)(2,1)}, s32[1,4]{1,0:T(1,128)}, s32[2]{0:T(128)S(1)}, f32[1,384]{1,0:T(1,128)S(1)}, ...), branch_computations={%region_0.1_spmd, %region_1.2_spmd, %region_2.3_spmd, %region_3.4_... | conditional | flops 3058016256 | bytes 16950642 | solution.py:238
  7.1 0.0 copy-start.4
  7.1 0.0 copy-start.11
  7.1 1.2 %copy.58 = bf16[1,2,16,24,384]{4,2,1,3,0:T(8,128)(2,1)S(1)} copy(bf16[1,2,16,24,384]{4,3,2,1,0:T(8,128)(2,1)} %get-tuple-element.145) | data formatting | bytes 1179648 | tf_op jit(solution)/shard_map
  8.3 3.1 %collective-permute-start.24 = (bf16[1,2,16,24,384]{4,2,1,3,0:T(8,128)(2,1)S(1)}, bf16[1,2,16,24,384]{4,2,1,3,0:T(8,128)(2,1)S(1)}, u32[]{:S(2)}, u32[]{:S(2)}) collective-permute-start(bf16[1,2,16,24,384]{4,2,1,3,0:T(8,128)(2,1)S(1)} %copy.58), channel_id=1, source_target_pairs={{0,128},{128,192},{192,64},{64,0},{1,129},{129,193},{193,65},{65,1... | collective-permute-start | bytes 1769480 | tf_op jit(solution)/shard_map/cond/branch_4_fun/ppermute | solution.py:210
  11.4 0.1 constant_dynamic-slice_fusion.4
  11.5 7.3 %collective-permute-start.20 = (bf16[2,24,384]{2,1,0:T(8,128)(2,1)S(1)}, bf16[2,24,384]{2,1,0:T(8,128)(2,1)S(1)}, u32[]{:S(2)}, u32[]{:S(2)}) collective-permute-start(bf16[2,24,384]{2,1,0:T(8,128)(2,1)S(1)} %bitcast.135), channel_id=1, source_target_pairs={{0,32},{2,34},{4,36},{6,38},{8,40},{10,42},{12,44},{14,46},{16,48}... | collective-permute-start | bytes 110600 | tf_op jit(solution)/shard_map/cond/branch_4_fun/ppermute | solution.py:214
  18.8 2.0 %collective-permute-done.20 = bf16[2,24,384]{2,1,0:T(8,128)(2,1)S(1)} collective-permute-done((bf16[2,24,384]{2,1,0:T(8,128)(2,1)S(1)}, bf16[2,24,384]{2,1,0:T(8,128)(2,1)S(1)}, u32[]{:S(2)}, u32[]{:S(2)}) %collective-permute-start.20) | collective-permute-done | bytes 36896 | tf_op jit(solution)/shard_map/cond/branch_4_fun/ppermute | solution.py:214
  20.8 2.6 %collective-permute-start.21 = (bf16[2,24,384]{2,1,0:T(8,128)(2,1)S(1)}, bf16[2,24,384]{2,1,0:T(8,128)(2,1)S(1)}, u32[]{:S(2)}, u32[]{:S(2)}) collective-permute-start(bf16[2,24,384]{2,1,0:T(8,128)(2,1)S(1)} %fusion.28), channel_id=1, source_target_pairs={{0,2},{2,4},{4,6},{6,8},{8,10},{10,12},{12,14},{14,16},{16,18},{18... | collective-permute-start | bytes 110600 | tf_op jit(solution)/shard_map/cond/branch_4_fun/ppermute | solution.py:223
  23.4 3.3 %collective-permute-start.22 = (bf16[2,24,384]{2,1,0:T(8,128)(2,1)S(1)}, bf16[2,24,384]{2,1,0:T(8,128)(2,1)S(1)}, u32[]{:S(2)}, u32[]{:S(2)}) collective-permute-start(bf16[2,24,384]{2,1,0:T(8,128)(2,1)S(1)} %fusion.29), channel_id=1, source_target_pairs={{2,0},{4,2},{6,4},{8,6},{10,8},{12,10},{14,12},{16,14},{18,16},{20... | collective-permute-start | bytes 110600 | tf_op jit(solution)/shard_map/cond/branch_4_fun/ppermute | solution.py:224
  26.7 0.0 collective-permute-done.21
  26.7 4.7 %collective-permute-done.22 = bf16[2,24,384]{2,1,0:T(8,128)(2,1)S(1)} collective-permute-done((bf16[2,24,384]{2,1,0:T(8,128)(2,1)S(1)}, bf16[2,24,384]{2,1,0:T(8,128)(2,1)S(1)}, u32[]{:S(2)}, u32[]{:S(2)}) %collective-permute-start.22) | collective-permute-done | bytes 36896 | tf_op jit(solution)/shard_map/cond/branch_4_fun/ppermute | solution.py:224
  31.4 1.7 %collective-permute-start.23 = (bf16[3,2,24,384]{3,2,1,0:T(8,128)(2,1)S(1)}, bf16[3,2,24,384]{3,2,1,0:T(8,128)(2,1)}, u32[]{:S(2)}, u32[]{:S(2)}) collective-permute-start(bf16[3,2,24,384]{3,2,1,0:T(8,128)(2,1)S(1)} %pad_maximum_fusion.4.halo), channel_id=1, source_target_pairs={{0,128},{128,192},{192,64},{64,0},{1,129},{129,193},{193,65},{65,1... | collective-permute-start | bytes 331784 | tf_op jit(solution)/shard_map/cond/branch_4_fun/ppermute | solution.py:226
  33.1 8.9 %branch_4_fun.1 = f32[2,384,384]{2,1,0:T(8,128)S(1)} custom-call(s32[1,4]{1,0:T(1,128)S(1)} %copy-done.11, s32[2]{0:T(128)S(1)} %get-tuple-element.105.where, bf16[768,384]{1,0:T(8,128)(2,1)S(1)} %bitcast.99, bf16[3,2,24,384]{3,2,1,0:T(8,128)(2,1)S(1)} %pad_maximum_fusion.4.halo, f32[1,384]{1,0:T(1,128)S(1)} %get-tuple-element.106.gain, ...), custom_call_target="tpu_custom_call" | custom-call | flops 3057647616 | bytes 8388608 | tf_op jit(solution)/shard_map/cond/branch_4_fun/pallas_call | solution.py:164
  42.0 0.0 collective-permute-done.24
  42.0 0.2 copy.21
  42.2 0.0 collective-permute-done.23
  46.4 10.1 %shard_map.64 = bf16[768,384]{1,0:T(8,128)(2,1)} custom-call(s32[1,4]{1,0:T(1,128)} %margins.1, s32[2]{0:T(128)S(1)} %pad_add_fusion.where, bf16[768,384]{1,0:T(8,128)(2,1)S(1)} %get-tuple-element.117.core, bf16[3,2,24,384]{3,2,1,0:T(8,128)(2,1)} %get-tuple-element.118.halo, f32[1,384]{1,0:T(1,128)S(1)} %reshape.47.gain, bf16[3,3456,384]{2,1,0:T(8,128)(2,1)} %bitcast.143, ...), custom_call_target="tpu_custom_call" | custom-call | flops 3057647616 | bytes 8388608 | tf_op jit(solution)/shard_map/pallas_call | solution.py:164
  (10 shorter events, 0.1 us)
Async XLA Ops:
  6.8 39.6 %copy-start.6 = (f32[384]{0:T(512)S(1)}, f32[384]{0:T(512)}, u32[]{:S(2)}) copy-start(f32[384]{0:T(512)} %param.17) | copy-start | bytes 4612
  7.1 26.1 %copy-start.4 = (bf16[1,2,16,24,384]{4,3,2,1,0:T(8,128)(2,1)S(1)}, bf16[1,2,16,24,384]{4,3,2,1,0:T(8,128)(2,1)}, u32[]{:S(2)}) copy-start(bf16[1,2,16,24,384]{4,3,2,1,0:T(8,128)(2,1)} %get-tuple-element.145) | copy-start | bytes 1769476 | tf_op jit(solution)/shard_map/cond
  7.1 26.0 %copy-start.11 = (s32[1,4]{1,0:T(1,128)S(1)}, s32[1,4]{1,0:T(1,128)}, u32[]{:S(2)}) copy-start(s32[1,4]{1,0:T(1,128)} %get-tuple-element.104.margins) | copy-start | bytes 52 | tf_op jit(solution)/shard_map/cond
  8.3 33.7 %collective-permute-start.24 = (bf16[1,2,16,24,384]{4,2,1,3,0:T(8,128)(2,1)S(1)}, bf16[1,2,16,24,384]{4,2,1,3,0:T(8,128)(2,1)S(1)}, u32[]{:S(2)}, u32[]{:S(2)}) collective-permute-start(bf16[1,2,16,24,384]{4,2,1,3,0:T(8,128)(2,1)S(1)} %copy.58), channel_id=1, source_target_pairs={{0,128},{128,192},{192,64},{64,0},{1,129},{129,193},{193,65},{65,1... | collective-permute-start | bytes 1769480 | tf_op jit(solution)/shard_map/cond/branch_4_fun/ppermute | solution.py:210
  11.5 9.3 %collective-permute-start.20 = (bf16[2,24,384]{2,1,0:T(8,128)(2,1)S(1)}, bf16[2,24,384]{2,1,0:T(8,128)(2,1)S(1)}, u32[]{:S(2)}, u32[]{:S(2)}) collective-permute-start(bf16[2,24,384]{2,1,0:T(8,128)(2,1)S(1)} %bitcast.135), channel_id=1, source_target_pairs={{0,32},{2,34},{4,36},{6,38},{8,40},{10,42},{12,44},{14,46},{16,48}... | collective-permute-start | bytes 110600 | tf_op jit(solution)/shard_map/cond/branch_4_fun/ppermute | solution.py:214
  20.8 5.9 %collective-permute-start.21 = (bf16[2,24,384]{2,1,0:T(8,128)(2,1)S(1)}, bf16[2,24,384]{2,1,0:T(8,128)(2,1)S(1)}, u32[]{:S(2)}, u32[]{:S(2)}) collective-permute-start(bf16[2,24,384]{2,1,0:T(8,128)(2,1)S(1)} %fusion.28), channel_id=1, source_target_pairs={{0,2},{2,4},{4,6},{6,8},{8,10},{10,12},{12,14},{14,16},{16,18},{18... | collective-permute-start | bytes 110600 | tf_op jit(solution)/shard_map/cond/branch_4_fun/ppermute | solution.py:223
  23.4 8.0 %collective-permute-start.22 = (bf16[2,24,384]{2,1,0:T(8,128)(2,1)S(1)}, bf16[2,24,384]{2,1,0:T(8,128)(2,1)S(1)}, u32[]{:S(2)}, u32[]{:S(2)}) collective-permute-start(bf16[2,24,384]{2,1,0:T(8,128)(2,1)S(1)} %fusion.29), channel_id=1, source_target_pairs={{2,0},{4,2},{6,4},{8,6},{10,8},{12,10},{14,12},{16,14},{18,16},{20... | collective-permute-start | bytes 110600 | tf_op jit(solution)/shard_map/cond/branch_4_fun/ppermute | solution.py:224
  31.4 10.9 %collective-permute-start.23 = (bf16[3,2,24,384]{3,2,1,0:T(8,128)(2,1)S(1)}, bf16[3,2,24,384]{3,2,1,0:T(8,128)(2,1)}, u32[]{:S(2)}, u32[]{:S(2)}) collective-permute-start(bf16[3,2,24,384]{3,2,1,0:T(8,128)(2,1)S(1)} %pad_maximum_fusion.4.halo), channel_id=1, source_target_pairs={{0,128},{128,192},{192,64},{64,0},{1,129},{129,193},{193,65},{65,1... | collective-permute-start | bytes 331784 | tf_op jit(solution)/shard_map/cond/branch_4_fun/ppermute | solution.py:226

commit v2 on v1

v2 whole, which is shorter than its diff:
```python
import jax
import jax.numpy as jnp
from jax import lax
from jax.experimental import pallas as pl
from jax.experimental.pallas import tpu as pltpu
from jax.sharding import PartitionSpec as P

GRID_R = 2
ROWS, COLS, C = 16, 24, 384
CELLS = ROWS * COLS
PAIR = 2 * COLS
DEPTH = 9 * C


def activated(values, half_gain):
    inv_norm = lax.rsqrt(jnp.mean(values * values, axis=-1, keepdims=True) + 1e-06)
    half = values * inv_norm * half_gain
    silu = half + half * jnp.tanh(half)
    return silu.astype(jnp.bfloat16).astype(jnp.float32)


def blend_coef(position, tap, core, near, far):
    source = position + (tap - 1)
    near_f, far_f = near.astype(jnp.float32), far.astype(jnp.float32)
    weight_near = jnp.maximum(near - position, 0).astype(jnp.float32) / (near_f + 1.0)
    weight_far = jnp.maximum(far + 1 - core + position, 0).astype(jnp.float32) / (far_f + 1.0)
    kept = jnp.where(source < near, weight_near, 0.0)
    kept = kept + jnp.where(source >= core - far, weight_far, 0.0)
    kept = kept + jnp.where((source >= -near) & (source < core + far), 1.0, 0.0)
    return kept / (weight_near + 1.0 + weight_far)


def shifted(block, left, right, coef_first, coef_last):
    size = block.shape[0]
    place = lax.broadcasted_iota(jnp.int32, (8, C), 0)
    before = pltpu.roll(block, 1, 0)
    after = pltpu.roll(block, size - 1, 0)
    before_parts, after_parts = [], []
    for n in range(size // COLS):
        first, middle, last = (slice(n * COLS + at, n * COLS + at + 8) for at in (0, 8, 16))
        before_parts += [
            jnp.where(place == 0, left[n], before[first]),
            before[middle],
            before[last] * coef_first,
        ]
        after_parts += [
            after[first] * coef_last,
            after[middle],
            jnp.where(place == 7, right[n], after[last]),
        ]
    return jnp.concatenate(before_parts, axis=0), block, jnp.concatenate(after_parts, axis=0)


def expand(margins, core, halo, gain, row_coefs, sides, spare, stacked, top, keep):
    place = lax.broadcasted_iota(jnp.int32, (8, C), 0)
    coef_first = blend_coef(place + (COLS - 8), 0, COLS, margins[0, 0], margins[0, 1])
    coef_last = blend_coef(place, 2, COLS, margins[0, 0], margins[0, 1])
    row = lax.broadcasted_iota(jnp.int32, (ROWS, C), 0)
    for n, b in enumerate((0, 2)):
        row_coefs[n] = blend_coef(row, b, ROWS, margins[0, 2], margins[0, 3])
    half_gain = 0.5 * gain
    if keep is not None:
        half_gain = jnp.where(keep, half_gain, 0.0)

    def frame(f, _):
        left = activated(halo[1, f].astype(jnp.float32), half_gain)
        right = activated(halo[2, f].astype(jnp.float32), half_gain)
        sides[0] = left
        sides[1] = right
        rim = activated(halo[0, f].astype(jnp.float32), half_gain)
        rims = shifted(
            rim, [left[ROWS : ROWS + 1]], [right[ROWS : ROWS + 1]], coef_first, coef_last
        )
        for e in range(3):
            spare[0, e] = jnp.where(top, rims[e], 0.0)
            spare[1, e] = jnp.where(top, 0.0, rims[e])

        def lanes(b, e):
            return slice((3 * b + e) * C, (3 * b + e + 1) * C)

        def two_rows(k, scale_above, scale_below, above):
            rows = pl.ds(pl.multiple_of(k * PAIR, 16), PAIR)
            block = core[pl.ds(pl.multiple_of(f * CELLS + k * PAIR, 16), PAIR), :]
            block = activated(block.astype(jnp.float32), half_gain)
            views = shifted(
                block,
                [sides[0, pl.ds(2 * k + n, 1), :] for n in range(2)],
                [sides[1, pl.ds(2 * k + n, 1), :] for n in range(2)],
                coef_first,
                coef_last,
            )
            for e in range(3):
                stacked[f, rows, lanes(1, e)] = views[e].astype(jnp.bfloat16)
                pieces = [spare[0, e], views[e][:COLS]]
                spare[0, e] = views[e][COLS:]

                def put(to, b, scale, first):
                    values = pieces
                    if scale:
                        values = [
                            p * row_coefs[b // 2, pl.ds(first + n, 1), :]
                            for n, p in enumerate(values)
                        ]
                    values = jnp.concatenate(values, axis=0).astype(jnp.bfloat16)
                    stacked[f, pl.ds(pl.multiple_of(to * PAIR, 16), PAIR), lanes(b, e)] = values

                put(k, 0, scale_above, 2 * k)
                if above:
                    put(k - 1, 2, scale_below, 2 * k - 2)

        def loop(first, last, scale_above, scale_below):
            def step(k, _):
                two_rows(k, scale_above, scale_below, True)
                return 0

            lax.fori_loop(first, last, step, 0)

        two_rows(0, False, False, False)
        loop(1, 3, False, True)
        loop(3, 6, False, False)
        loop(6, 8, True, False)
        for e in range(3):
            values = jnp.concatenate([spare[0, e], spare[1, e]], axis=0).astype(jnp.bfloat16)
            stacked[f, (ROWS - 2) * COLS : ROWS * COLS, lanes(2, e)] = values
        return 0

    lax.fori_loop(0, 2, frame, 0)


def fetch(weights, taps, sems, first, second):
    copies = [
        pltpu.make_async_copy(weights.at[a], taps.at[:, pl.ds(n * C, C)], sems.at[n])
        for n, a in enumerate((first, second))
    ]
    for copy in copies:
        copy.start()
    return copies


def dot(a, b):
    return jnp.dot(a, b, preferred_element_type=jnp.float32)


def own_kernel(
    margins, tile_row, core, halo, gain, weights, out, taps, row_coefs, sides, spare, stacked, sems
):
    copies = fetch(weights, taps, sems, 2, 1)
    gain = gain[...].reshape(1, C)
    expand(margins, core, halo, gain, row_coefs, sides, spare, stacked, tile_row[0] == 1, None)
    for copy in copies:
        copy.wait()

    def part(n, _):
        rows = pl.ds(pl.multiple_of(n * 128, 16), 128)
        both = dot(stacked[0, rows, :], taps[...])
        out[0, rows, :] = both[:, :C]
        out[1, rows, :] = both[:, C:] + dot(stacked[1, rows, :], taps[:, :C])
        return 0

    lax.fori_loop(0, CELLS // 128, part, 0)


def previous_kernel(
    margins,
    tile_row,
    core,
    halo,
    gain,
    weights,
    own,
    bias,
    slot,
    out,
    taps,
    row_coefs,
    sides,
    spare,
    stacked,
    sems,
):
    copies = fetch(weights, taps, sems, 1, 0)
    gain = gain[...].reshape(1, C)
    bias = bias[...].reshape(1, C)
    expand(
        margins, core, halo, gain, row_coefs, sides, spare, stacked, tile_row[0] == 1, slot[0] > 0
    )
    for copy in copies:
        copy.wait()
    both = dot(stacked[1], taps[...])
    first = own[0] + bias + both[:, :C] + dot(stacked[0], taps[:, C:])
    out[0:CELLS] = first.astype(jnp.bfloat16)
    out[CELLS : 2 * CELLS] = (own[1] + bias + both[:, C:]).astype(jnp.bfloat16)


SMEM, VMEM, HBM = (pl.BlockSpec(memory_space=m) for m in (pltpu.SMEM, pltpu.VMEM, pl.ANY))


def call(kernel, inputs, specs, out_shape):
    return pl.pallas_call(
        kernel,
        in_specs=specs,
        out_specs=VMEM,
        out_shape=out_shape,
        scratch_shapes=[
            pltpu.VMEM((DEPTH, 2 * C), jnp.bfloat16),
            pltpu.VMEM((2, ROWS, C), jnp.float32),
            pltpu.VMEM((2, COLS, C), jnp.float32),
            pltpu.VMEM((2, 3, COLS, C), jnp.float32),
            pltpu.VMEM((2, CELLS, DEPTH), jnp.bfloat16),
            pltpu.SemaphoreType.DMA((2,)),
        ],
        compiler_params=pltpu.CompilerParams(vmem_limit_bytes=40 * 2**20),
        cost_estimate=pl.CostEstimate(
            flops=2 * 3 * CELLS * DEPTH * C, bytes_accessed=8 * 2**20, transcendentals=2 * CELLS * C
        ),
    )(*inputs)


def prepare_kernel(group_slot, tile_row, core, index, rim, columns):
    away = [(group_slot[d] - group_slot[0] + 4) % 4 for d in (1, 2, 3)]
    index[0] = (away[0] - 1) * 2 + jnp.where(away[1] > away[2], 1, 0)
    top = tile_row[0] == 1
    for f in range(2):
        blocks = [
            core[f * CELLS + k * PAIR : f * CELLS + (k + 1) * PAIR].astype(jnp.float32)
            for k in range(ROWS // 2)
        ]
        rim[f] = jnp.where(top, blocks[0][:COLS], blocks[-1][COLS:]).astype(jnp.bfloat16)
        for side, at in enumerate((0, COLS - 1)):
            cells = [block[at + n : at + n + 1] for block in blocks for n in (0, COLS)]
            columns[side, f] = jnp.concatenate(cells, axis=0).astype(jnp.bfloat16)


def prepare(group_slot, tile_row, core):
    return pl.pallas_call(
        prepare_kernel,
        in_specs=[SMEM, SMEM, VMEM],
        out_specs=[SMEM, VMEM, VMEM],
        out_shape=[
            jax.ShapeDtypeStruct((1,), jnp.int32),
            jax.ShapeDtypeStruct((2, COLS, C), jnp.bfloat16),
            jax.ShapeDtypeStruct((2, 2, ROWS, C), jnp.bfloat16),
        ],
    )(group_slot, tile_row, core)


def cyclic_order(index):
    place = index // 2 + 1
    others = [p for p in (1, 2, 3) if p != place]
    if index % 2:
        others = others[::-1]
    places = [0, place] + others
    return sorted(range(4), key=lambda d: places[d])


def local(features, group_slot, margins, norm_gain, kernel, conv_bias):
    tiles = lax.axis_size("tile")
    across = tiles // GRID_R
    tile_row = (lax.axis_index("tile") // across).astype(jnp.int32).reshape(1)
    slot = group_slot[lax.axis_index("group")].reshape(1)
    weights = kernel.reshape(3, DEPTH, C)
    core = features.reshape(2 * CELLS, C)
    index, edge, edge_columns = prepare(group_slot, tile_row, core)

    def routed(order):
        route = [(order[n], order[(n + 1) % 4]) for n in range(4)]

        def branch(features, edge, edge_columns, tile_row, margins, gain, weights):
            previous = lax.ppermute(features, "group", route)
            rim = lax.ppermute(edge, "tile", [(t, (t + across) % tiles) for t in range(tiles)])
            spare = jnp.zeros((2, COLS - ROWS - 1, C), jnp.bfloat16)
            first, last = (
                jnp.concatenate([edge_columns[side], rim[:, at : at + 1], spare], axis=1)
                for side, at in ((0, 0), (1, COLS - 1))
            )
            inner = [t for t in range(tiles) if t % across != across - 1]
            left = lax.ppermute(last, "tile", [(t, t + 1) for t in inner])
            right = lax.ppermute(first, "tile", [(t + 1, t) for t in inner])
            halo = jnp.stack([rim, left, right])
            halo_previous = lax.ppermute(halo, "group", route)
            partial = call(
                own_kernel,
                (margins, tile_row, features.reshape(2 * CELLS, C), halo, gain, weights),
                [SMEM, SMEM, VMEM, VMEM, VMEM, HBM],
                jax.ShapeDtypeStruct((2, CELLS, C), jnp.float32),
            )
            return previous, halo_previous, partial

        return branch

    previous, halo_previous, partial = lax.switch(
        index[0],
        [routed(cyclic_order(n)) for n in range(6)],
        features,
        edge,
        edge_columns,
        tile_row,
        margins,
        norm_gain,
        weights,
    )
    decoded = call(
        previous_kernel,
        (
            margins,
            tile_row,
            previous.reshape(2 * CELLS, C),
            halo_previous,
            norm_gain,
            weights,
            partial,
            conv_bias,
            slot,
        ),
        [SMEM, SMEM, VMEM, VMEM, VMEM, HBM, VMEM, VMEM, SMEM],
        jax.ShapeDtypeStruct((2 * CELLS, C), jnp.bfloat16),
    )
    return decoded.reshape(1, 2, ROWS, COLS, C)


def solution(mesh):
    return jax.shard_map(
        local,
        mesh=mesh,
        in_specs=(
            P(("video", "tile"), "group", None, None, None),
            P(),
            P("tile", None),
            P(),
            P(),
            P(),
        ),
        out_specs=P(("video", "tile"), "group", None, None, None),
        check_vma=False,
    )
```

time: 57.6 us -> 44.3 us (0.77); the launches traced: 56.7 us -> 44.2 us
  loops' own time: 4.49 us -> 0.5 us
  local copies, waits for them, and re-layouts: 4.25 us -> 1.42 us
  other arithmetic: 2.18 us -> 0.1 us
  waiting for transfers between devices: 6.66 us -> 4.7 us
  between operations: 2.15 us -> 0.86 us
    another operation x1, loops' own time: 4.49 us -> 0.5 us  [local(): lax.switch(index[0], [routed(cyclic_order(n)) for n in range(6)], feature...]
    slice x2 -> x0, local copies, waits for them, and re-layouts: 2.05 us -> none  [the longest x1 1.39 us: local(): away = (group_slot[1:] - group_slot[0]) % 4]
    ppermute x1, waiting for transfers between devices: 1.97 us -> 0.01 us  [branch(): lax.ppermute(edge, 'tile', [(t, (t + across) % tiles) for t in range(tile...]
    select_n x1 -> x0, other arithmetic: 1.38 us -> none  [local(): away = (group_slot[1:] - group_slot[0]) % 4]
    dynamic_slice x2 -> x1, local copies, waits for them, and re-layouts: 0.09 us -> 1.32 us  [local(): slot = group_slot[lax.axis_index('group')].reshape(1)]
    another operation x1, local copies, waits for them, and re-layouts: 1.2 us -> 0.01 us
    another operation x1 -> x0, other arithmetic: 0.76 us -> none  [local(): where = jnp.stack([tile_row, slot]).astype(jnp.int32)]
    reshape x2 -> x0, local copies, waits for them, and re-layouts: 0.69 us -> none  [the longest x1 0.68 us: local(): gain = norm_gain.reshape(1, C)]
  transfers between devices with their start and end apart: 5 -> 5, of which waited for: 2 -> 1; matrix products, arithmetic and copies ran while one was open for 1% -> 0% of each run, Pallas kernels for 16% -> 18%
where the time goes in v2:
time: 44.3 us; the launch traced here: 44.2 us
  Pallas kernels  18.5 us (42%)
  starting transfers between devices  18.1 us (41%)
  waiting for transfers between devices  4.7 us (11%)
  local copies, waits for them, and re-layouts  1.42 us (3%)
  between operations  0.86 us (2%)
  loops' own time  0.5 us (1%)
    pallas_call x2, Pallas kernels, call(): pl.pallas_call(kernel, in_specs=specs, out_specs=VMEM, out_shape=out_shap...  16.9 us
    ppermute x1, starting transfers between devices, branch(): lax.ppermute(edge, 'tile', [(t, (t + across) % tiles) for t in range(tile...  7.28 us
    ppermute x1, waiting for transfers between devices, branch(): right = lax.ppermute(first, 'tile', [(t + 1, t) for t in inner])  4.69 us
    ppermute x1, starting transfers between devices, branch(): right = lax.ppermute(first, 'tile', [(t + 1, t) for t in inner])  3.26 us
    ppermute x1, starting transfers between devices, branch(): previous = lax.ppermute(features, 'group', route)  3.02 us
    ppermute x1, starting transfers between devices, branch(): left = lax.ppermute(last, 'tile', [(t, t + 1) for t in inner])  2.59 us
    ppermute x1, starting transfers between devices, branch(): halo_previous = lax.ppermute(halo, 'group', route)  1.93 us
    pallas_call x1, Pallas kernels, prepare(): pl.pallas_call(prepare_kernel, in_specs=[SMEM, SMEM, VMEM], out_specs=[SM...  1.61 us
  transfers between devices with their start and end apart: 5, of which 1 were waited for; matrix products, arithmetic and copies ran while one was open for 0% of the time, Pallas kernels for 18%

profile of v2, /device:TPU:24, one launch (start us, length us, event | category | flops | bytes accessed | tf_op | source)
XLA Modules:
  0.0 44.2 jit_solution(3196780272412897562)
XLA Ops:
  0.0 1.3 %dynamic_slice.3.slot = s32[1]{0:T(128)} dynamic-slice(s32[4]{0:T(128)} %group_slot.1, s32[]{:T(128)S(6)} %select_n.9), dynamic_slice_sizes={1} | dynamic-slice | bytes 12 | tf_op jit(solution)/shard_map/dynamic_slice | solution.py:260
  1.3 1.6 %shard_map.64 = (s32[1]{0:T(128)}, bf16[2,24,384]{2,1,0:T(8,128)(2,1)S(1)}, bf16[2,2,16,384]{3,2,1,0:T(8,128)(2,1)S(1)}) custom-call(s32[4]{0:T(128)} %group_slot.1, s32[1]{0:T(128)} %bitcast.42.tile_row, bf16[768,384]{1,0:T(8,128)(2,1)} %bitcast.59), custom_call_target="tpu_custom_call" | custom-call | tf_op jit(solution)/shard_map/pallas_call | solution.py:235
  3.6 0.0 copy-start
  3.6 31.4 %conditional.1 = (bf16[3,2,24,384]{3,2,1,0:T(8,128)(2,1)}, f32[2,384,384]{2,1,0:T(8,128)S(1)}, bf16[768,384]{1,0:T(8,128)(2,1)}) conditional(s32[]{:T(128)} %bitcast.44, (bf16[2,24,384]{2,1,0:T(8,128)(2,1)S(1)}, bf16[2,2,16,384]{3,2,1,0:T(8,128)(2,1)S(1)}, bf16[1,2,16,24,384]{4,3,2,1,0:T(8,128)(2,1)}, ...), branch_computations={%region_0.1_spmd, %region_1.2_spmd, %region_2.3_spmd, %region_3.4_... | conditional | flops 3057960960 | bytes 12084576 | solution.py:291
  3.6 7.3 %collective-permute-start.10 = (bf16[2,24,384]{2,1,0:T(8,128)(2,1)S(1)}, bf16[2,24,384]{2,1,0:T(8,128)(2,1)S(1)}, u32[]{:S(2)}, u32[]{:S(2)}) collective-permute-start(bf16[2,24,384]{2,1,0:T(8,128)(2,1)S(1)} %get-tuple-element.104), channel_id=1, source_target_pairs={{0,32},{2,34},{4,36},{6,38},{8,40},{10,42},{12,44},{14,46},{16,48}... | collective-permute-start | bytes 110600 | tf_op jit(solution)/shard_map/cond/branch_2_fun/ppermute | solution.py:270
  10.9 3.0 %collective-permute-start.14 = (bf16[1,2,16,24,384]{4,3,2,1,0:T(8,128)(2,1)}, bf16[1,2,16,24,384]{4,3,2,1,0:T(8,128)(2,1)}, u32[]{:S(2)}, u32[]{:S(2)}) collective-permute-start(bf16[1,2,16,24,384]{4,3,2,1,0:T(8,128)(2,1)} %get-tuple-element.108), channel_id=1, source_target_pairs={{0,128},{128,64},{64,192},{192,0},{1,129},{129,65},{65,193},{193,1... | collective-permute-start | bytes 1769480 | tf_op jit(solution)/shard_map/cond/branch_2_fun/ppermute | solution.py:269
  13.9 0.1 pad.26.clone
  14.0 0.0 collective-permute-done.10
  14.0 0.1 maximum_maximum_fusion.4
  14.1 2.6 %collective-permute-start.11 = (bf16[2,24,384]{2,1,0:T(8,128)(2,1)S(1)}, bf16[2,24,384]{2,1,0:T(8,128)(2,1)S(1)}, u32[]{:S(2)}, u32[]{:S(2)}) collective-permute-start(bf16[2,24,384]{2,1,0:T(8,128)(2,1)S(1)} %get-tuple-element.160), channel_id=1, source_target_pairs={{0,2},{2,4},{4,6},{6,8},{8,10},{10,12},{12,14},{14,16},{16,18},{18... | collective-permute-start | bytes 110600 | tf_op jit(solution)/shard_map/cond/branch_2_fun/ppermute | solution.py:277
  16.7 3.3 %collective-permute-start.12 = (bf16[2,24,384]{2,1,0:T(8,128)(2,1)S(1)}, bf16[2,24,384]{2,1,0:T(8,128)(2,1)S(1)}, u32[]{:S(2)}, u32[]{:S(2)}) collective-permute-start(bf16[2,24,384]{2,1,0:T(8,128)(2,1)S(1)} %get-tuple-element.161), channel_id=1, source_target_pairs={{2,0},{4,2},{6,4},{8,6},{10,8},{12,10},{14,12},{16,14},{18,16},{20... | collective-permute-start | bytes 110600 | tf_op jit(solution)/shard_map/cond/branch_2_fun/ppermute | solution.py:278
  20.0 0.0 collective-permute-done.11
  20.0 4.7 %collective-permute-done.12 = bf16[2,24,384]{2,1,0:T(8,128)(2,1)S(1)} collective-permute-done((bf16[2,24,384]{2,1,0:T(8,128)(2,1)S(1)}, bf16[2,24,384]{2,1,0:T(8,128)(2,1)S(1)}, u32[]{:S(2)}, u32[]{:S(2)}) %collective-permute-start.12) | collective-permute-done | bytes 36896 | tf_op jit(solution)/shard_map/cond/branch_2_fun/ppermute | solution.py:278
  24.7 1.9 %collective-permute-start.13 = (bf16[3,2,24,384]{3,2,1,0:T(8,128)(2,1)S(1)}, bf16[3,2,24,384]{3,2,1,0:T(8,128)(2,1)}, u32[]{:S(2)}, u32[]{:S(2)}) collective-permute-start(bf16[3,2,24,384]{3,2,1,0:T(8,128)(2,1)S(1)} %pad_maximum_fusion.2.halo), channel_id=1, source_target_pairs={{0,128},{128,64},{64,192},{192,0},{1,129},{129,65},{65,193},{193,1... | collective-permute-start | bytes 331784 | tf_op jit(solution)/shard_map/cond/branch_2_fun/ppermute | solution.py:280
  26.6 8.0 %branch_2_fun.1 = f32[2,384,384]{2,1,0:T(8,128)S(1)} custom-call(s32[1,4]{1,0:T(1,128)} %get-tuple-element.106.margins, s32[1]{0:T(128)} %get-tuple-element.107.tile_row, bf16[768,384]{1,0:T(8,128)(2,1)} %bitcast.62, bf16[3,2,24,384]{3,2,1,0:T(8,128)(2,1)S(1)} %pad_maximum_fusion.2.halo, f32[384]{0:T(512)} %get-tuple-element.109.gain, ...), custom_call_target="tpu_custom_call" | custom-call | flops 3057647616 | bytes 8388608 | tf_op jit(solution)/shard_map/cond/branch_2_fun/pallas_call | solution.py:199
  34.6 0.0 collective-permute-done.13
  34.6 0.0 collective-permute-done.14
  35.0 0.0 copy-done
  35.0 9.0 %shard_map.65 = bf16[768,384]{1,0:T(8,128)(2,1)} custom-call(s32[1,4]{1,0:T(1,128)} %margins.1, s32[1]{0:T(128)} %bitcast.42.tile_row, bf16[768,384]{1,0:T(8,128)(2,1)} %get-tuple-element.141.core, bf16[3,2,24,384]{3,2,1,0:T(8,128)(2,1)} %get-tuple-element.142.halo, f32[384]{0:T(512)} %gain.1, bf16[3,3456,384]{2,1,0:T(8,128)(2,1)} %bitcast.90, ...), custom_call_target="tpu_custom_call" | custom-call | flops 3057647616 | bytes 8388608 | tf_op jit(solution)/shard_map/pallas_call | solution.py:199
  (4 shorter events, 0.0 us)
Async XLA Ops:
  3.6 31.5 %copy-start = (f32[384]{0:T(512)S(1)}, f32[384]{0:T(512)}, u32[]{:S(2)}) copy-start(f32[384]{0:T(512)} %bias.1) | copy-start | bytes 4612
  3.6 10.4 %collective-permute-start.10 = (bf16[2,24,384]{2,1,0:T(8,128)(2,1)S(1)}, bf16[2,24,384]{2,1,0:T(8,128)(2,1)S(1)}, u32[]{:S(2)}, u32[]{:S(2)}) collective-permute-start(bf16[2,24,384]{2,1,0:T(8,128)(2,1)S(1)} %get-tuple-element.104), channel_id=1, source_target_pairs={{0,32},{2,34},{4,36},{6,38},{8,40},{10,42},{12,44},{14,46},{16,48}... | collective-permute-start | bytes 110600 | tf_op jit(solution)/shard_map/cond/branch_2_fun/ppermute | solution.py:270
  10.9 23.7 %collective-permute-start.14 = (bf16[1,2,16,24,384]{4,3,2,1,0:T(8,128)(2,1)}, bf16[1,2,16,24,384]{4,3,2,1,0:T(8,128)(2,1)}, u32[]{:S(2)}, u32[]{:S(2)}) collective-permute-start(bf16[1,2,16,24,384]{4,3,2,1,0:T(8,128)(2,1)} %get-tuple-element.108), channel_id=1, source_target_pairs={{0,128},{128,64},{64,192},{192,0},{1,129},{129,65},{65,193},{193,1... | collective-permute-start | bytes 1769480 | tf_op jit(solution)/shard_map/cond/branch_2_fun/ppermute | solution.py:269
  14.1 5.9 %collective-permute-start.11 = (bf16[2,24,384]{2,1,0:T(8,128)(2,1)S(1)}, bf16[2,24,384]{2,1,0:T(8,128)(2,1)S(1)}, u32[]{:S(2)}, u32[]{:S(2)}) collective-permute-start(bf16[2,24,384]{2,1,0:T(8,128)(2,1)S(1)} %get-tuple-element.160), channel_id=1, source_target_pairs={{0,2},{2,4},{4,6},{6,8},{8,10},{10,12},{12,14},{14,16},{16,18},{18... | collective-permute-start | bytes 110600 | tf_op jit(solution)/shard_map/cond/branch_2_fun/ppermute | solution.py:277
  16.7 8.0 %collective-permute-start.12 = (bf16[2,24,384]{2,1,0:T(8,128)(2,1)S(1)}, bf16[2,24,384]{2,1,0:T(8,128)(2,1)S(1)}, u32[]{:S(2)}, u32[]{:S(2)}) collective-permute-start(bf16[2,24,384]{2,1,0:T(8,128)(2,1)S(1)} %get-tuple-element.161), channel_id=1, source_target_pairs={{2,0},{4,2},{6,4},{8,6},{10,8},{12,10},{14,12},{16,14},{18,16},{20... | collective-permute-start | bytes 110600 | tf_op jit(solution)/shard_map/cond/branch_2_fun/ppermute | solution.py:278
  24.7 9.9 %collective-permute-start.13 = (bf16[3,2,24,384]{3,2,1,0:T(8,128)(2,1)S(1)}, bf16[3,2,24,384]{3,2,1,0:T(8,128)(2,1)}, u32[]{:S(2)}, u32[]{:S(2)}) collective-permute-start(bf16[3,2,24,384]{3,2,1,0:T(8,128)(2,1)S(1)} %pad_maximum_fusion.2.halo), channel_id=1, source_target_pairs={{0,128},{128,64},{64,192},{192,0},{1,129},{129,65},{65,193},{193,1... | collective-permute-start | bytes 331784 | tf_op jit(solution)/shard_map/cond/branch_2_fun/ppermute | solution.py:280
